TPU v7x, 32 devices: a whole 2x2x4 slice. The times are simulated.
32 devices in a mesh: groups: 2 (over x), epoch: 4 (over y, core), space: 4 (over z).
Axes of the slice: x: 2, y: 2, z: 4, core: 2. Of those that a mesh axis runs over, the one named last changes fastest.
Arguments:
- slc_stack: bfloat16 [2, 32, 32, 960], P(None, ('epoch', 'space'), 'groups'), parts along dimension 2, may hold values from -45 to 45
Outputs:
- coherence: bfloat16 [2, 32, 32, 2048], P(None, 'epoch', None, ('groups', 'space')), parts along dimension 3
There are 2 independent parts, one for each index of `groups`. A program takes and returns all parts, laid end to end along the dimension named above; each array names one. Nothing has to cross between parts.
All inputs are finite; a program needn't handle non-finite values.
Results may differ from a plain program's by a relative error of at most 0.001.
Values may be sent and summed in bfloat16 or wider, within the bound.
A program may use at most 128 MiB of HBM per device.

v0:
```python
import functools

import jax
import jax.numpy as jnp
from jax import lax
from jax.experimental import pallas as pl
from jax.experimental.pallas import tpu as pltpu
from jax.sharding import PartitionSpec as P

LOOKR = 5
LOOKC = 15
MARGIN = 2
LANES = 128
MESH = pl.DeviceIdType.MESH
F32 = jnp.float32
BF16 = jnp.bfloat16


def iota(shape, axis):
    return lax.broadcasted_iota(jnp.int32, shape, axis)


def one_hot(hits):
    return jnp.where(hits, 1.0, 0.0).astype(BF16)


def over(value, by):
    return value >> (by.bit_length() - 1) if by & (by - 1) == 0 else lax.div(value, by)


def rest(value, by):
    return value & (by - 1) if by & (by - 1) == 0 else lax.rem(value, by)


def kernel(dims, x_hbm, got, x_ref, cut, mid_out, edge_out, mid_in, edge_in, *rest_refs):
    n_epoch, n_space, local, rows, cols, strip, pieces, mid_rows, edge_rows = dims
    mid_order, edge_order, fold, lefts, epochs, folded, middle, coh = rest_refs[:8]
    load, send_mid, recv_mid, send_edge, recv_edge, send_coh, recv_coh = rest_refs[8:]
    total = n_epoch * n_space * local
    block = n_space * local
    held = strip + 2 * MARGIN
    width = cols // n_epoch
    part = width // pieces
    looks = width // LOOKC
    looks_part = looks // pieces
    planes = 2 * pieces
    lanes = block * looks
    my_i = lax.axis_index("epoch")
    my_j = lax.axis_index("space")
    me = my_i * n_space + my_j

    def epoch_peer(step):
        core = lax.rem(lax.rem(my_i, 2) + step % 2, 2)
        return lax.rem(my_i // 2 + step // 2, n_epoch // 2) * 2 + core

    def epoch_source(step):
        core = lax.rem(lax.rem(my_i, 2) + step % 2, 2)
        return lax.rem(my_i // 2 + n_epoch // 2 - step // 2, n_epoch // 2) * 2 + core

    steps = [
        (a, b)
        for b in reversed(range(n_space))
        for a in reversed(range(n_epoch))
        if a or b
    ]
    targets = [(epoch_peer(a), lax.rem(my_j + b, n_space)) for a, b in steps]
    origins = [(epoch_source(a), lax.rem(my_j + n_space - b, n_space)) for a, b in steps]

    loading = pltpu.make_async_copy(x_hbm, x_ref, load)
    loading.start()
    barrier = pltpu.get_barrier_semaphore()
    for to_i, to_j in targets:
        pl.semaphore_signal(
            barrier,
            inc=1,
            device_id={"epoch": to_i, "space": to_j},
            device_id_type=MESH,
        )

    def picker(count, size, sides, first):
        shape = (n_space * sides * size, planes * local * rows)
        goal, held_at = iota(shape, 0), iota(shape, 1)
        spot = rest(goal, size)
        row = over(spot, planes * local)
        wanted = over(goal, sides * size) * strip + row + first(rest(over(goal, size), sides))
        return one_hot(
            (row < count)
            & (rest(spot, planes) == over(held_at, local * rows))
            & (rest(over(spot, planes), local) == rest(over(held_at, rows), local))
            & (wanted == rest(held_at, rows))
        )

    pick = jnp.concatenate(
        [
            picker(strip, mid_rows, 1, lambda side: 0),
            picker(
                MARGIN, edge_rows, 2, lambda side: jnp.where(side == 0, -MARGIN, strip)
            ),
        ],
        axis=0,
    )
    loading.wait()
    for k in range(2):
        image = x_ref[k].reshape(local * rows, cols).astype(F32)
        for i in range(n_epoch):
            for h in range(pieces):
                start = i * width + h * part
                piece = image[:, start : start + part]
                if part < LANES:
                    blank = jnp.zeros((local * rows, LANES - part), F32)
                    piece = jnp.concatenate([piece, blank], axis=1)
                plane = k * pieces + h
                cut[
                    plane * local * rows : (plane + 1) * local * rows,
                    i * LANES : (i + 1) * LANES,
                ] = piece.astype(BF16)
    picked = jnp.dot(pick, cut[...], preferred_element_type=F32).astype(BF16)
    for i in range(n_epoch):
        side = slice(i * LANES, (i + 1) * LANES)
        for j in range(n_space):
            mid_out[i * n_space + j] = picked[j * mid_rows : (j + 1) * mid_rows, side]
            for z in range(2):
                start = n_space * mid_rows + (2 * j + z) * edge_rows
                edge_out[i * n_space + j, z] = picked[start : start + edge_rows, side]

    pl.semaphore_wait(barrier, len(steps))

    def mid_copy(slot, to_i, to_j, source):
        return pltpu.make_async_remote_copy(
            src_ref=mid_out.at[to_i * n_space + to_j],
            dst_ref=mid_in.at[source],
            send_sem=send_mid.at[slot],
            recv_sem=recv_mid.at[source],
            device_id={"epoch": to_i, "space": to_j},
            device_id_type=MESH,
        )

    def edge_copy(slot, to_i, to_j, source, low, count):
        return pltpu.make_async_remote_copy(
            src_ref=edge_out.at[to_i * n_space + to_j, pl.ds(low, count)],
            dst_ref=edge_in.at[source, pl.ds(low, count)],
            send_sem=send_edge.at[slot],
            recv_sem=recv_edge.at[source],
            device_id={"epoch": to_i, "space": to_j},
            device_id_type=MESH,
        )

    def by_place(j, act):
        if n_space > 1:
            pl.when(j == 0)(lambda: act(1, 1))
            pl.when(j == n_space - 1)(lambda: act(0, 1))
            pl.when((j > 0) & (j < n_space - 1))(lambda: act(0, 2))

    for slot, (to_i, to_j) in enumerate(targets):
        mid_copy(slot, to_i, to_j, me).start()
    for slot, (to_i, to_j) in enumerate(targets):
        by_place(
            to_j,
            lambda low, count: edge_copy(slot, to_i, to_j, me, low, count).start(),
        )

    @pl.when(my_j == 0)
    def _():
        edge_in[:, 0] = jnp.zeros((n_epoch * n_space, edge_rows, LANES), BF16)

    @pl.when(my_j == n_space - 1)
    def _():
        edge_in[:, 1] = jnp.zeros((n_epoch * n_space, edge_rows, LANES), BF16)

    mid_in[me] = mid_out[me]
    edge_in[me] = edge_out[me]

    def order(count, size):
        shape = (planes * count * total, n_epoch * n_space * size)
        goal, fro = iota(shape, 0), iota(shape, 1)
        spot = rest(fro, size)
        row = over(spot, planes * local)
        epoch = over(fro, size) * local + rest(over(spot, planes), local)
        want = (rest(spot, planes) * count + row) * total + epoch
        return one_hot((row < count) & (goal == want))

    mid_order[...] = order(strip, mid_rows)
    edge_order[...] = order(MARGIN, edge_rows)
    lane = iota((pieces * LANES, lanes), 0)
    look = rest(iota((pieces * LANES, lanes), 1), looks) - over(lane, LANES) * looks_part
    spare = rest(lane, LANES) - look * LOOKC
    fold[...] = jnp.where((spare >= 0) & (spare < LOOKC), 1.0, 0.0)
    lane = iota((1, looks, planes * LANES), 2)
    look = iota((1, looks, planes * LANES), 1) - rest(over(lane, LANES), pieces) * looks_part
    spare = rest(lane, LANES) - look * LOOKC
    inside = (spare >= 0) & (spare < LOOKC)
    own_lane = over(iota((block, lanes), 1), looks) == iota((block, lanes), 0)

    def settle(order_ref, arrived, held_rows):
        count = len(held_rows)
        sorted_rows = jnp.dot(order_ref[...], arrived, preferred_element_type=F32)
        size = count * total
        whole = [sorted_rows[p * size : (p + 1) * size] for p in range(planes)]
        re = jnp.concatenate(whole[:pieces], axis=1)
        im = jnp.concatenate(whole[pieces:], axis=1)
        plain = jnp.concatenate([re, im], axis=1)
        turned = jnp.concatenate([-im, re], axis=1)
        sums = jnp.dot(
            re * re + im * im,
            fold[...],
            preferred_element_type=F32,
            precision=lax.Precision.HIGHEST,
        )
        for n, row in enumerate(held_rows):
            part_of = slice(n * total, (n + 1) * total)
            epochs[row] = plain[part_of]
            factor = jnp.concatenate([plain[part_of], turned[part_of]], axis=0)
            lefts[row] = factor.T.astype(BF16)
            folded[row] = sums[part_of]

    def place_of(group):
        first = group * block
        return pl.ds(pl.multiple_of(first, 8) if block % 8 == 0 else first, block)

    def gram(row, images):
        masked = jnp.where(inside, images[:, None, :], 0.0).astype(BF16)
        masked = masked.reshape(images.shape[0] * looks, planes * LANES)
        return jnp.dot(masked, lefts[row], preferred_element_type=F32)

    def add_up(terms):
        return functools.reduce(lambda p, q: p + q, terms)

    own_rows = list(range(MARGIN, MARGIN + strip))
    edge_sides = [list(range(MARGIN)), list(range(MARGIN + strip, held))]
    windows = [range(r, r + LOOKR) for r in range(strip)]

    for slot, (from_i, from_j) in enumerate(origins):
        mid_copy(slot, from_i, from_j, from_i * n_space + from_j).wait_recv()
    settle(mid_order, mid_in[...].reshape(n_epoch * n_space * mid_rows, LANES), own_rows)
    for group in range(n_epoch):
        share = slice(group * block, (group + 1) * block)
        grams = {row: gram(row, epochs[row, share, :]) for row in own_rows}
        for r in range(strip):
            middle[group, r] = add_up([grams[row] for row in windows[r] if row in grams])

    for slot, (from_i, from_j) in enumerate(origins):
        by_place(
            my_j,
            lambda low, count: edge_copy(
                slot, from_i, from_j, from_i * n_space + from_j, low, count
            ).wait_recv(),
        )
    for z in range(2):
        arrived = edge_in[:, z].reshape(n_epoch * n_space * edge_rows, LANES)
        settle(edge_order, arrived, edge_sides[z])

    def coh_copy(slot, to_i, source):
        return pltpu.make_async_remote_copy(
            src_ref=coh.at[slot],
            dst_ref=got.at[source],
            send_sem=send_coh.at[slot],
            recv_sem=recv_coh.at[source],
            device_id={"epoch": to_i},
            device_id_type=MESH,
        )

    for step in reversed(range(n_epoch)):
        to_i = epoch_peer(step)
        grams = {
            row: gram(row, epochs[row, place_of(to_i), :])
            for rows_of in edge_sides
            for row in rows_of
        }
        for r in range(strip):
            cross = middle[to_i, r] + add_up([grams[row] for row in windows[r] if row in grams])
            cross = cross.T
            power = add_up([folded[row] for row in windows[r]]) + 1e-06
            left = add_up([folded[row, place_of(to_i), :] for row in windows[r]]) + 1e-06
            left = jnp.sum(jnp.where(own_lane, left, 0.0), axis=0, keepdims=True)
            inverse = lax.rsqrt(left * power)
            value = jnp.concatenate(
                [cross[:total] * inverse, cross[total:] * inverse], axis=0
            ).astype(BF16)
            if step:
                coh[step, r] = value
            else:
                got[my_i, r] = value
        if step:
            coh_copy(step, to_i, my_i).start()

    for step in reversed(range(1, n_epoch)):
        from_i = epoch_source(step)
        coh_copy(step, from_i, from_i).wait_recv()
    for step in range(1, n_epoch):
        coh_copy(step, epoch_peer(step), my_i).wait_send()
    for slot, (to_i, to_j) in enumerate(targets):
        mid_copy(slot, to_i, to_j, me).wait_send()
        by_place(
            to_j,
            lambda low, count: edge_copy(slot, to_i, to_j, me, low, count).wait_send(),
        )


def spread_kernel(dims, got, out_hbm, out_ref, sem):
    n_epoch, block, total, strip, all_looks = dims
    looks = all_looks // n_epoch
    lanes = block * looks
    if lanes == LANES and (strip * n_epoch) % block == 0 and block & (block - 1) == 0:
        spot = over(iota((2 * total, lanes), 1), looks)
        copies = []
        for half in range(strip * n_epoch // block):
            tiles = []
            for t in range(half * block, (half + 1) * block):
                tiles.append(got[t % n_epoch, t // n_epoch].astype(F32))
            bit = 1
            while bit < block:
                low = spot & bit == 0
                turned_tiles = list(tiles)
                for t in range(block):
                    if t & bit:
                        continue
                    one, two = tiles[t], tiles[t + bit]
                    turned_tiles[t] = jnp.where(low, one, pltpu.roll(two, bit * looks, 1))
                    turned_tiles[t + bit] = jnp.where(
                        low, pltpu.roll(one, lanes - bit * looks, 1), two
                    )
                tiles = turned_tiles
                bit *= 2
            for e in range(block):
                value = tiles[e].astype(BF16)
                for k in range(2):
                    out_ref[k, e, :, half * lanes : (half + 1) * lanes] = value[
                        k * total : (k + 1) * total
                    ]
            side = pl.ds(half * lanes, lanes)
            copies.append(
                pltpu.make_async_copy(
                    out_ref.at[:, :, :, side], out_hbm.at[:, :, :, side], sem.at[half]
                )
            )
            copies[-1].start()
        for copy in copies:
            copy.wait()
    else:
        shape = (lanes, strip * all_looks)
        fro_e, fro_c, goal = iota(shape, 0) // looks, iota(shape, 0) % looks, iota(shape, 1)
        for e in range(block):

            def add(i, acc):
                for r in range(strip):
                    spread = one_hot((fro_e == e) & (goal == r * all_looks + i * looks + fro_c))
                    acc = acc + jnp.dot(got[i, r], spread, preferred_element_type=F32)
                return acc

            value = lax.fori_loop(0, n_epoch, add, jnp.zeros((2 * total, shape[1]), F32))
            value = value.astype(BF16)
            for k in range(2):
                out_ref[k, e] = value[k * total : (k + 1) * total]
        whole = pltpu.make_async_copy(out_ref, out_hbm, sem.at[0])
        whole.start()
        whole.wait()


def per_device(slc_stack):
    n_epoch, n_space = lax.axis_size("epoch"), lax.axis_size("space")
    _, local, rows, cols = slc_stack.shape
    strip = rows // n_space
    held = strip + 2 * MARGIN
    total = n_epoch * n_space * local
    block = n_space * local
    width = cols // n_epoch
    looks = width // LOOKC
    all_looks = cols // LOOKC
    lanes = block * looks
    pieces = next(p for p in range(1, looks + 1) if looks % p == 0 and width // p <= LANES)
    planes = 2 * pieces
    mid_rows = -(-strip * local * planes // 16) * 16
    edge_rows = -(-MARGIN * local * planes // 16) * 16
    sources = n_epoch * n_space
    dims = (n_epoch, n_space, local, rows, cols, strip, pieces, mid_rows, edge_rows)
    vmem = pl.BlockSpec(memory_space=pltpu.VMEM)
    hbm = pl.BlockSpec(memory_space=pl.ANY)
    got = pl.pallas_call(
        functools.partial(kernel, dims),
        out_shape=jax.ShapeDtypeStruct((n_epoch, strip, 2 * total, lanes), BF16),
        in_specs=[hbm],
        out_specs=vmem,
        scratch_shapes=[
            pltpu.VMEM(slc_stack.shape, BF16),
            pltpu.VMEM((planes * local * rows, n_epoch * LANES), BF16),
            pltpu.VMEM((sources, mid_rows, LANES), BF16),
            pltpu.VMEM((sources, 2, edge_rows, LANES), BF16),
            pltpu.VMEM((sources, mid_rows, LANES), BF16),
            pltpu.VMEM((sources, 2, edge_rows, LANES), BF16),
            pltpu.VMEM((planes * strip * total, sources * mid_rows), BF16),
            pltpu.VMEM((planes * MARGIN * total, sources * edge_rows), BF16),
            pltpu.VMEM((pieces * LANES, lanes), F32),
            pltpu.VMEM((held, planes * LANES, 2 * total), BF16),
            pltpu.VMEM((held, total, planes * LANES), F32),
            pltpu.VMEM((held, total, lanes), F32),
            pltpu.VMEM((n_epoch, strip, lanes, 2 * total), F32),
            pltpu.VMEM((n_epoch, strip, 2 * total, lanes), BF16),
            pltpu.SemaphoreType.DMA(()),
            pltpu.SemaphoreType.DMA((sources - 1,)),
            pltpu.SemaphoreType.DMA((sources,)),
            pltpu.SemaphoreType.DMA((sources - 1,)),
            pltpu.SemaphoreType.DMA((sources,)),
            pltpu.SemaphoreType.DMA((n_epoch,)),
            pltpu.SemaphoreType.DMA((n_epoch,)),
        ],
        compiler_params=pltpu.CompilerParams(
            collective_id=0, has_side_effects=True, vmem_limit_bytes=48 * 1024 * 1024
        ),
        cost_estimate=pl.CostEstimate(flops=10**9, bytes_accessed=10**6, transcendentals=0),
    )(pltpu.with_memory_space_constraint(slc_stack, pltpu.HBM))
    out = jax.ShapeDtypeStruct((2, block, total, strip * all_looks), BF16)
    return pl.pallas_call(
        functools.partial(spread_kernel, (n_epoch, block, total, strip, all_looks)),
        out_shape=out,
        in_specs=[vmem],
        out_specs=hbm,
        scratch_shapes=[
            pltpu.VMEM(out.shape, BF16),
            pltpu.SemaphoreType.DMA((max(1, strip * n_epoch // block),)),
        ],
        compiler_params=pltpu.CompilerParams(vmem_limit_bytes=32 * 1024 * 1024),
    )(got)


def solution(mesh):
    in_specs = (P(None, ("epoch", "space"), "groups", None),)
    out_specs = P(None, "epoch", None, ("groups", "space"))
    return jax.shard_map(
        per_device, mesh=mesh, in_specs=in_specs, out_specs=out_specs, check_vma=False
    )
```

profile of v0, /device:TPU:0, one launch (start us, length us, event | category | flops | bytes accessed | tf_op | source)
XLA Modules:
  0.0 20.0 jit_solution(8322875055917958541)
XLA Ops:
  0.0 18.9 %shard_map.17.got = bf16[4,4,64,128]{3,2,1,0:T(8,128)(2,1)S(1)} custom-call(bf16[2,2,16,960]{3,2,1,0:T(8,128)(2,1)} %x_hbm.1), custom_call_target="tpu_custom_call" | custom-call | flops 1000000000 | bytes 1000000 | tf_op jit(solution)/shard_map/pallas_call | solution.py:378
  18.9 1.1 %shard_map.18 = bf16[2,8,32,256]{3,2,1,0:T(8,128)(2,1)} custom-call(bf16[4,4,64,128]{3,2,1,0:T(8,128)(2,1)S(1)} %shard_map.17.got), custom_call_target="tpu_custom_call" | custom-call | tf_op jit(solution)/shard_map/pallas_call | solution.py:412
where the time goes:
time: 20.1 us; the launch traced here: 20 us
  Pallas kernels  20 us (100%)
    pallas_call x1, Pallas kernels, per_device(): pl.pallas_call(functools.partial(kernel, dims), out_shape=jax.ShapeDtypeS...  18.9 us
    pallas_call x1, Pallas kernels, per_device(): pl.pallas_call(functools.partial(spread_kernel, (n_epoch, block, total, s...  1.09 us

commit v1 on v0

v1 whole, which is shorter than its diff:
```python
import functools

import jax
import jax.numpy as jnp
from jax import lax
from jax.experimental import pallas as pl
from jax.experimental.pallas import tpu as pltpu
from jax.sharding import PartitionSpec as P

LOOKR = 5
LOOKC = 15
MARGIN = 2
LANES = 128
MESH = pl.DeviceIdType.MESH
F32 = jnp.float32
BF16 = jnp.bfloat16


def iota(shape, axis):
    return lax.broadcasted_iota(jnp.int32, shape, axis)


def one_hot(hits):
    return jnp.where(hits, 1.0, 0.0).astype(BF16)


def over(value, by):
    return value >> (by.bit_length() - 1) if by & (by - 1) == 0 else lax.div(value, by)


def rest(value, by):
    return value & (by - 1) if by & (by - 1) == 0 else lax.rem(value, by)


def kernel(dims, x_hbm, got, x_ref, cut, strips, parts, *rest_refs):
    n_epoch, n_space, local, rows, cols, strip, pieces, size = dims
    order, fold, lefts, epochs, folded, middle, coh = rest_refs[:7]
    load, send_strip, recv_strip, send_coh, recv_coh = rest_refs[7:]
    total = n_epoch * n_space * local
    block = n_space * local
    held = strip + 2 * MARGIN
    chunks = held // MARGIN
    width = cols // n_epoch
    part = width // pieces
    looks = width // LOOKC
    looks_part = looks // pieces
    planes = 2 * pieces
    lanes = block * looks
    my_i = lax.axis_index("epoch")
    my_j = lax.axis_index("space")
    me = my_i * n_space + my_j

    def epoch_peer(step):
        core = lax.rem(lax.rem(my_i, 2) + step % 2, 2)
        return lax.rem(my_i // 2 + step // 2, n_epoch // 2) * 2 + core

    def epoch_source(step):
        core = lax.rem(lax.rem(my_i, 2) + step % 2, 2)
        return lax.rem(my_i // 2 + n_epoch // 2 - step // 2, n_epoch // 2) * 2 + core

    steps = [
        (a, b)
        for b in reversed(range(n_space))
        for a in reversed(range(n_epoch))
        if a or b
    ]
    targets = [(epoch_peer(a), lax.rem(my_j + b, n_space)) for a, b in steps]
    origins = [(epoch_source(a), lax.rem(my_j + n_space - b, n_space)) for a, b in steps]

    loading = pltpu.make_async_copy(x_hbm, x_ref, load)
    loading.start()
    barrier = pltpu.get_barrier_semaphore()
    for to_i, to_j in targets:
        pl.semaphore_signal(
            barrier,
            inc=1,
            device_id={"epoch": to_i, "space": to_j},
            device_id_type=MESH,
        )

    shape = (n_space * chunks * size, planes * local * rows)
    goal, held_at = iota(shape, 0), iota(shape, 1)
    spot = rest(goal, size)
    row = over(spot, planes * local)
    first = over(goal, chunks * size) * strip - MARGIN
    wanted = first + rest(over(goal, size), chunks) * MARGIN + row
    pick = one_hot(
        (row < MARGIN)
        & (rest(spot, planes) == over(held_at, local * rows))
        & (rest(over(spot, planes), local) == rest(over(held_at, rows), local))
        & (wanted == rest(held_at, rows))
    )
    loading.wait()
    for k in range(2):
        image = x_ref[k].reshape(local * rows, cols).astype(F32)
        for i in range(n_epoch):
            for h in range(pieces):
                start = i * width + h * part
                piece = image[:, start : start + part]
                if part < LANES:
                    blank = jnp.zeros((local * rows, LANES - part), F32)
                    piece = jnp.concatenate([piece, blank], axis=1)
                plane = k * pieces + h
                cut[
                    plane * local * rows : (plane + 1) * local * rows,
                    i * LANES : (i + 1) * LANES,
                ] = piece.astype(BF16)
    picked = jnp.dot(pick, cut[...], preferred_element_type=F32).astype(BF16)
    for i in range(n_epoch):
        side = slice(i * LANES, (i + 1) * LANES)
        for j in range(n_space):
            for z in range(chunks):
                start = (j * chunks + z) * size
                strips[i * n_space + j, z] = picked[start : start + size, side]

    pl.semaphore_wait(barrier, len(steps))

    def strip_copy(part, slot, to_i, to_j, source, low, count):
        return pltpu.make_async_remote_copy(
            src_ref=strips.at[to_i * n_space + to_j, pl.ds(low, count)],
            dst_ref=parts.at[source, pl.ds(low, count)],
            send_sem=send_strip.at[part, slot],
            recv_sem=recv_strip.at[part, source],
            device_id={"epoch": to_i, "space": to_j},
            device_id_type=MESH,
        )

    def by_place(part, j, act):
        if part == 0:
            pl.when(j == 0)(lambda: act(1, chunks - 2))
            pl.when(j > 0)(lambda: act(0, chunks - 1))
        else:
            pl.when(j < n_space - 1)(lambda: act(chunks - 1, 1))

    for part_of in range(2):
        for slot, (to_i, to_j) in enumerate(targets):
            by_place(
                part_of,
                to_j,
                lambda low, count: strip_copy(
                    part_of, slot, to_i, to_j, me, low, count
                ).start(),
            )

    @pl.when(my_j == 0)
    def _():
        parts[:, 0] = jnp.zeros((n_epoch * n_space, size, LANES), BF16)

    @pl.when(my_j == n_space - 1)
    def _():
        parts[:, chunks - 1] = jnp.zeros((n_epoch * n_space, size, LANES), BF16)

    parts[me] = strips[me]

    shape = (planes * MARGIN * total, n_epoch * n_space * size)
    goal, fro = iota(shape, 0), iota(shape, 1)
    spot = rest(fro, size)
    row = over(spot, planes * local)
    epoch = over(fro, size) * local + rest(over(spot, planes), local)
    want = (rest(spot, planes) * MARGIN + row) * total + epoch
    order[...] = one_hot((row < MARGIN) & (goal == want))
    lane = iota((pieces * LANES, lanes), 0)
    look = rest(iota((pieces * LANES, lanes), 1), looks) - over(lane, LANES) * looks_part
    spare = rest(lane, LANES) - look * LOOKC
    fold[...] = jnp.where((spare >= 0) & (spare < LOOKC), 1.0, 0.0)
    lane = iota((1, looks, planes * LANES), 2)
    look = iota((1, looks, planes * LANES), 1) - rest(over(lane, LANES), pieces) * looks_part
    spare = rest(lane, LANES) - look * LOOKC
    inside = (spare >= 0) & (spare < LOOKC)
    own_lane = over(iota((block, lanes), 1), looks) == iota((block, lanes), 0)

    def settle(chunk):
        arrived = parts[:, chunk].reshape(n_epoch * n_space * size, LANES)
        sorted_rows = jnp.dot(order[...], arrived, preferred_element_type=F32)
        many = MARGIN * total
        whole = [sorted_rows[p * many : (p + 1) * many] for p in range(planes)]
        re = jnp.concatenate(whole[:pieces], axis=1)
        im = jnp.concatenate(whole[pieces:], axis=1)
        plain = jnp.concatenate([re, im], axis=1)
        turned = jnp.concatenate([-im, re], axis=1)
        sums = jnp.dot(
            re * re + im * im,
            fold[...],
            preferred_element_type=F32,
            precision=lax.Precision.HIGHEST,
        )
        for n in range(MARGIN):
            row = chunk * MARGIN + n
            part_of = slice(n * total, (n + 1) * total)
            epochs[row] = plain[part_of]
            factor = jnp.concatenate([plain[part_of], turned[part_of]], axis=0)
            lefts[row] = factor.T.astype(BF16)
            folded[row] = sums[part_of]

    def place_of(group):
        first = group * block
        return pl.ds(pl.multiple_of(first, 8) if block % 8 == 0 else first, block)

    def gram(row, images):
        masked = jnp.where(inside, images[:, None, :], 0.0).astype(BF16)
        masked = masked.reshape(images.shape[0] * looks, planes * LANES)
        return jnp.dot(masked, lefts[row], preferred_element_type=F32)

    def add_up(terms):
        return functools.reduce(lambda p, q: p + q, terms)

    windows = [range(r, r + LOOKR) for r in range(strip)]
    known = held - MARGIN
    early = [r for r in range(strip) if r + LOOKR <= known]
    late = [r for r in range(strip) if r + LOOKR > known]
    halves = [(early[0], len(early)), (late[0], len(late))]

    def coh_copy(half, slot, to_i, source):
        start, count = halves[half]
        return pltpu.make_async_remote_copy(
            src_ref=coh.at[slot, pl.ds(start, count)],
            dst_ref=got.at[source, pl.ds(start, count)],
            send_sem=send_coh.at[half, slot],
            recv_sem=recv_coh.at[half, source],
            device_id={"epoch": to_i},
            device_id_type=MESH,
        )

    def finish(cross, r, to_i):
        power = add_up([folded[row] for row in windows[r]]) + 1e-06
        left = add_up([folded[row, place_of(to_i), :] for row in windows[r]]) + 1e-06
        left = jnp.sum(jnp.where(own_lane, left, 0.0), axis=0, keepdims=True)
        inverse = lax.rsqrt(left * power)
        cross = cross.T
        return jnp.concatenate(
            [cross[:total] * inverse, cross[total:] * inverse], axis=0
        ).astype(BF16)

    for half, (chunk_list, row_list) in enumerate(
        [
            (range(chunks - 1), range(known)),
            (range(chunks - 1, chunks), range(known, held)),
        ]
    ):
        for slot, (from_i, from_j) in enumerate(origins):
            by_place(
                half,
                my_j,
                lambda low, count: strip_copy(
                    half, slot, from_i, from_j, from_i * n_space + from_j, low, count
                ).wait_recv(),
            )
        for chunk in chunk_list:
            settle(chunk)
        for step in reversed(range(n_epoch)):
            to_i = epoch_peer(step)
            grams = {row: gram(row, epochs[row, place_of(to_i), :]) for row in row_list}
            for r in early if half == 0 else late:
                cross = add_up([grams[row] for row in windows[r] if row in grams])
                if half:
                    cross = cross + middle[to_i, r - late[0]]
                value = finish(cross, r, to_i)
                if step:
                    coh[step, r] = value
                else:
                    got[my_i, r] = value
            if step:
                coh_copy(half, step, to_i, my_i).start()
            if half == 0:
                for r in late:
                    middle[to_i, r - late[0]] = add_up(
                        [grams[row] for row in windows[r] if row in grams]
                    )

    for half in range(2):
        for step in reversed(range(1, n_epoch)):
            from_i = epoch_source(step)
            coh_copy(half, step, from_i, from_i).wait_recv()
    for half in range(2):
        for step in range(1, n_epoch):
            coh_copy(half, step, epoch_peer(step), my_i).wait_send()
        for slot, (to_i, to_j) in enumerate(targets):
            by_place(
                half,
                to_j,
                lambda low, count: strip_copy(
                    half, slot, to_i, to_j, me, low, count
                ).wait_send(),
            )


def spread_kernel(dims, got, out_hbm, out_ref, sem):
    n_epoch, block, total, strip, all_looks = dims
    looks = all_looks // n_epoch
    lanes = block * looks
    if lanes == LANES and (strip * n_epoch) % block == 0 and block & (block - 1) == 0:
        spot = over(iota((2 * total, lanes), 1), looks)
        copies = []
        for half in range(strip * n_epoch // block):
            tiles = []
            for t in range(half * block, (half + 1) * block):
                tiles.append(got[t % n_epoch, t // n_epoch].astype(F32))
            bit = 1
            while bit < block:
                low = spot & bit == 0
                turned_tiles = list(tiles)
                for t in range(block):
                    if t & bit:
                        continue
                    one, two = tiles[t], tiles[t + bit]
                    turned_tiles[t] = jnp.where(low, one, pltpu.roll(two, bit * looks, 1))
                    turned_tiles[t + bit] = jnp.where(
                        low, pltpu.roll(one, lanes - bit * looks, 1), two
                    )
                tiles = turned_tiles
                bit *= 2
            for e in range(block):
                value = tiles[e].astype(BF16)
                for k in range(2):
                    out_ref[k, e, :, half * lanes : (half + 1) * lanes] = value[
                        k * total : (k + 1) * total
                    ]
            side = pl.ds(half * lanes, lanes)
            copies.append(
                pltpu.make_async_copy(
                    out_ref.at[:, :, :, side], out_hbm.at[:, :, :, side], sem.at[half]
                )
            )
            copies[-1].start()
        for copy in copies:
            copy.wait()
    else:
        shape = (lanes, strip * all_looks)
        fro_e, fro_c, goal = iota(shape, 0) // looks, iota(shape, 0) % looks, iota(shape, 1)
        for e in range(block):

            def add(i, acc):
                for r in range(strip):
                    spread = one_hot((fro_e == e) & (goal == r * all_looks + i * looks + fro_c))
                    acc = acc + jnp.dot(got[i, r], spread, preferred_element_type=F32)
                return acc

            value = lax.fori_loop(0, n_epoch, add, jnp.zeros((2 * total, shape[1]), F32))
            value = value.astype(BF16)
            for k in range(2):
                out_ref[k, e] = value[k * total : (k + 1) * total]
        whole = pltpu.make_async_copy(out_ref, out_hbm, sem.at[0])
        whole.start()
        whole.wait()


def per_device(slc_stack):
    n_epoch, n_space = lax.axis_size("epoch"), lax.axis_size("space")
    _, local, rows, cols = slc_stack.shape
    strip = rows // n_space
    held = strip + 2 * MARGIN
    total = n_epoch * n_space * local
    block = n_space * local
    width = cols // n_epoch
    looks = width // LOOKC
    all_looks = cols // LOOKC
    lanes = block * looks
    pieces = next(p for p in range(1, looks + 1) if looks % p == 0 and width // p <= LANES)
    planes = 2 * pieces
    size = -(-MARGIN * local * planes // 16) * 16
    chunks = held // MARGIN
    sources = n_epoch * n_space
    dims = (n_epoch, n_space, local, rows, cols, strip, pieces, size)
    vmem = pl.BlockSpec(memory_space=pltpu.VMEM)
    hbm = pl.BlockSpec(memory_space=pl.ANY)
    got = pl.pallas_call(
        functools.partial(kernel, dims),
        out_shape=jax.ShapeDtypeStruct((n_epoch, strip, 2 * total, lanes), BF16),
        in_specs=[hbm],
        out_specs=vmem,
        scratch_shapes=[
            pltpu.VMEM(slc_stack.shape, BF16),
            pltpu.VMEM((planes * local * rows, n_epoch * LANES), BF16),
            pltpu.VMEM((sources, chunks, size, LANES), BF16),
            pltpu.VMEM((sources, chunks, size, LANES), BF16),
            pltpu.VMEM((planes * MARGIN * total, sources * size), BF16),
            pltpu.VMEM((pieces * LANES, lanes), F32),
            pltpu.VMEM((held, planes * LANES, 2 * total), BF16),
            pltpu.VMEM((held, total, planes * LANES), F32),
            pltpu.VMEM((held, total, lanes), F32),
            pltpu.VMEM((n_epoch, MARGIN, lanes, 2 * total), F32),
            pltpu.VMEM((n_epoch, strip, 2 * total, lanes), BF16),
            pltpu.SemaphoreType.DMA(()),
            pltpu.SemaphoreType.DMA((2, sources - 1)),
            pltpu.SemaphoreType.DMA((2, sources)),
            pltpu.SemaphoreType.DMA((2, n_epoch)),
            pltpu.SemaphoreType.DMA((2, n_epoch)),
        ],
        compiler_params=pltpu.CompilerParams(
            collective_id=0, has_side_effects=True, vmem_limit_bytes=48 * 1024 * 1024
        ),
        cost_estimate=pl.CostEstimate(flops=10**9, bytes_accessed=10**6, transcendentals=0),
    )(pltpu.with_memory_space_constraint(slc_stack, pltpu.HBM))
    out = jax.ShapeDtypeStruct((2, block, total, strip * all_looks), BF16)
    return pl.pallas_call(
        functools.partial(spread_kernel, (n_epoch, block, total, strip, all_looks)),
        out_shape=out,
        in_specs=[vmem],
        out_specs=hbm,
        scratch_shapes=[
            pltpu.VMEM(out.shape, BF16),
            pltpu.SemaphoreType.DMA((max(1, strip * n_epoch // block),)),
        ],
        compiler_params=pltpu.CompilerParams(vmem_limit_bytes=32 * 1024 * 1024),
    )(got)


def solution(mesh):
    in_specs = (P(None, ("epoch", "space"), "groups", None),)
    out_specs = P(None, "epoch", None, ("groups", "space"))
    return jax.shard_map(
        per_device, mesh=mesh, in_specs=in_specs, out_specs=out_specs, check_vma=False
    )
```

time: 20.1 us -> 20.6 us (1.025)
  Pallas kernels: 20 us -> 20.5 us
    pallas_call x1, Pallas kernels: 18.9 us -> 19.4 us  [per_device(): pl.pallas_call(functools.partial(kernel, dims), out_shape=jax.ShapeDtypeS...]
where the time goes in v1:
time: 20.6 us; the launch traced here: 20.5 us
  Pallas kernels  20.5 us (100%)
    pallas_call x1, Pallas kernels, per_device(): pl.pallas_call(functools.partial(kernel, dims), out_shape=jax.ShapeDtypeS...  19.4 us
    pallas_call x1, Pallas kernels, per_device(): pl.pallas_call(functools.partial(spread_kernel, (n_epoch, block, total, s...  1.09 us

profile of v1, /device:TPU:0, one launch (start us, length us, event | category | flops | bytes accessed | tf_op | source)
XLA Modules:
  0.0 20.5 jit_solution(6413613700451053386)
XLA Ops:
  0.0 19.4 %shard_map.17.got = bf16[4,4,64,128]{3,2,1,0:T(8,128)(2,1)S(1)} custom-call(bf16[2,2,16,960]{3,2,1,0:T(8,128)(2,1)} %x_hbm.1), custom_call_target="tpu_custom_call" | custom-call | flops 1000000000 | bytes 1000000 | tf_op jit(solution)/shard_map/pallas_call | solution.py:366
  19.4 1.1 %shard_map.18 = bf16[2,8,32,256]{3,2,1,0:T(8,128)(2,1)} custom-call(bf16[4,4,64,128]{3,2,1,0:T(8,128)(2,1)S(1)} %shard_map.17.got), custom_call_target="tpu_custom_call" | custom-call | tf_op jit(solution)/shard_map/pallas_call | solution.py:395
